TPU v7x, 32 devices: a whole 2x2x4 slice. The times are simulated.
32 devices in a mesh: layer: 2 (over y), row: 4 (over z), col: 4 (over x, core).
Axes of the slice: x: 2, y: 2, z: 4, core: 2. Of those that a mesh axis runs over, the one named last changes fastest.
Arguments:
- factor: float32 [32, 4, 256, 2048], P('layer', 'row', None, 'col'), parts along dimension 0, may hold values from -1 to 4, as said below
- gradient: bfloat16 [32, 4, 256, 4096], P('layer', 'row', None, 'col'), parts along dimension 0, may hold values from -6 to 6
Outputs:
- solution: float32 [32, 4, 256, 4096], P('layer', 'row', None, 'col'), parts along dimension 0
There are 2 independent parts, one for each index of `layer`. A program takes and returns all parts, laid end to end along the dimension named above; each array names one. Nothing has to cross between parts.
Inputs may be any that keep to these rules, and one draw needn't show every extreme that they name: The factor is lower triangular: the entry of whole row i and column j is zero for j > i, and the diagonal lies between 1 and 4.
All inputs are finite; a program needn't handle non-finite values.
Results may differ from a plain program's by a relative error of at most 0.0039.
Values may be sent and summed in bfloat16 or wider, within the bound.
A program may use at most 128 MiB of HBM per device.

v0:
```python
import jax
import jax.numpy as jnp
from jax import lax
from jax.sharding import PartitionSpec as P

STEPS = 8


def broadcast(shard, axis, root):
    mine = lax.axis_index(axis) == root
    return lax.psum(jnp.where(mine, shard, jnp.zeros_like(shard)), axis)


def local(factor, gradient):
    row_count = lax.axis_size("row")
    my_row = lax.axis_index("row")
    cycles, _, block_size, width_local = factor.shape
    blocks_per = width_local // block_size
    lowered = factor.reshape(cycles * block_size, width_local).astype(jnp.bfloat16)
    current = gradient.reshape(cycles * block_size, gradient.shape[3]).astype(jnp.float32)
    row_blocks = jnp.arange(cycles * block_size, dtype=jnp.int32) // block_size * row_count + my_row

    def fetch_tile(position):
        own_part = lax.dynamic_slice_in_dim(
            lowered, position % blocks_per * block_size, block_size, 1
        )
        return broadcast(own_part, "col", position // blocks_per)

    def own_rows(array, position):
        return lax.dynamic_slice_in_dim(array, position // row_count * block_size, block_size, 0)

    def solve_at(position, column_tile, right_side):
        diagonal = own_rows(column_tile, position).astype(jnp.float32)
        is_owner = position % row_count == my_row
        diagonal = jnp.where(is_owner, diagonal, jnp.eye(block_size, dtype=jnp.float32))
        return lax.linalg.triangular_solve(diagonal, right_side, left_side=True, lower=True)

    def share(solved, position):
        return broadcast(solved.astype(jnp.bfloat16), "row", position % row_count)

    def apply_block(current, position, column_tile, solved, sent_block):
        stored = lax.dynamic_update_slice_in_dim(
            current, solved, position // row_count * block_size, 0
        )
        is_owner = position % row_count == my_row
        current = jnp.where(is_owner, stored, current)
        product = jnp.dot(column_tile, sent_block, preferred_element_type=jnp.float32)
        pending = (row_blocks > position)[:, None]
        return current - jnp.where(pending, product, 0.0)

    def advance(position, current):
        column_tile = fetch_tile(position)
        solved = solve_at(position, column_tile, own_rows(current, position))
        sent_block = share(solved, position)
        return apply_block(current, position, column_tile, solved, sent_block)

    current = lax.fori_loop(0, STEPS, advance, current)
    return current.reshape(gradient.shape)


def solution(mesh):
    return jax.shard_map(
        local,
        mesh=mesh,
        in_specs=(P("layer", "row", None, "col"), P("layer", "row", None, "col")),
        out_specs=P("layer", "row", None, "col"),
        check_vma=False,
    )
```

profile of v0, /device:TPU:0, one launch (start us, length us, event | category | flops | bytes accessed | tf_op | source)
XLA Modules:
  0.0 1116.6 jit_solution(18060171137867233325)
XLA Ops:
  6.5 11.7 %bitcast_convert_fusion = f32[4096,1024]{1,0:T(8,128)} fusion(bf16[16,1,256,1024]{3,2,1,0:T(8,128)(2,1)} %param.5), kind=kLoop, calls=%fused_computation.31 | loop fusion | flops 4194304 | bytes 25165824 | tf_op jit(solution)/shard_map/convert_element_type | solution.py:20
  18.2 5.9 convert_element_type.47
  24.1 1085.9 %while.23 = (s32[]{:T(128)}, f32[4096,1024]{1,0:T(8,128)}, s32[]{:T(128)}, bf16[4096,512]{1,0:T(8,128)(2,1)}, s32[]{:T(128)}, /*index=5*/s32[]{:T(128)}, s32[]{:...) while((s32[]{:T(128)}, f32[4096,1024]{1,0:T(8,128)}, ...), condition=%wide.region_3.4_spmd.clone.clone, body=%wide.region_0.3_spmd.clone.clone.sunk | while | flops 2764615680 | bytes 65217368 | solution.py:57
  24.1 3.3 dynamic-slice_select_fusion.2
  27.6 54.1 %all-reduce.3.cloned.1.call-done = bf16[4096,256]{1,0:T(8,128)(2,1)} async-done(((bf16[4096,256]{1,0:T(8,128)(2,1)}), bf16[4096,256]{1,0:T(8,128)(2,1)}) %all-reduce.3.cloned.1.call-update) | async-done | bytes 2097168 | tf_op jit(solution)/shard_map/while/body/eval_jaxpr/psum | solution.py:11
  82.7 3.9 while.24
  86.6 19.7 %custom-call.17 = f32[2,128,128]{1,2,0:T(8,128)S(1)} custom-call(f32[2,128,128]{2,1,0:T(8,128)S(1)} %get-tuple-element.282), custom_call_target="InvertDiagBlocksLowerTriangular" | custom-call | tf_op jit(solution)/shard_map/while/body/eval_jaxpr/triangular_solve | solution.py:36
  106.3 1.7 fusion.37
  111.2 2.3 select_dynamic-update-slice_fusion.2
  113.6 36.2 %all-reduce.5.cloned.1.call-done = bf16[256,1024]{1,0:T(8,128)(2,1)} async-done(((bf16[256,1024]{1,0:T(8,128)(2,1)}), bf16[256,1024]{1,0:T(8,128)(2,1)}) %all-reduce.5.cloned.1.call-update) | async-done | bytes 524304 | tf_op jit(solution)/shard_map/while/body/eval_jaxpr/psum | solution.py:11
  149.8 12.5 %select_subtract_fusion.2 = f32[4096,1024]{1,0:T(8,128)} fusion(f32[4096,1024]{1,0:T(8,128)} %select_dynamic-update-slice_fusion.2, bf16[4096,256]{1,0:T(8,128)(2,1)} %all-reduce.3.cloned.1.call-done, bf16[256,1024]{1,0:T(8,128)(2,1)} %all-reduce.5.cloned.1.call-done, pred[4096]{0:T(1024)(128)(4,1)S(1)} %fusion.40), kind=kOutput, calls=%fused_computation.3.clone.1 | convolution fusion | flops 2155872256 | bytes 36179968 | tf_op jit(solution)/shard_map/while/body/eval_jaxpr/dot_general | solution.py:47
  162.3 3.3 dynamic-slice_select_fusion.2
  165.7 51.4 %all-reduce.3.cloned.1.call-done = bf16[4096,256]{1,0:T(8,128)(2,1)} async-done(((bf16[4096,256]{1,0:T(8,128)(2,1)}), bf16[4096,256]{1,0:T(8,128)(2,1)}) %all-reduce.3.cloned.1.call-update) | async-done | bytes 2097168 | tf_op jit(solution)/shard_map/while/body/eval_jaxpr/psum | solution.py:11
  218.1 3.9 while.24
  222.0 19.7 %custom-call.17 = f32[2,128,128]{1,2,0:T(8,128)S(1)} custom-call(f32[2,128,128]{2,1,0:T(8,128)S(1)} %get-tuple-element.282), custom_call_target="InvertDiagBlocksLowerTriangular" | custom-call | tf_op jit(solution)/shard_map/while/body/eval_jaxpr/triangular_solve | solution.py:36
  241.7 1.7 fusion.37
  246.6 2.3 select_dynamic-update-slice_fusion.2
  249.0 36.2 %all-reduce.5.cloned.1.call-done = bf16[256,1024]{1,0:T(8,128)(2,1)} async-done(((bf16[256,1024]{1,0:T(8,128)(2,1)}), bf16[256,1024]{1,0:T(8,128)(2,1)}) %all-reduce.5.cloned.1.call-update) | async-done | bytes 524304 | tf_op jit(solution)/shard_map/while/body/eval_jaxpr/psum | solution.py:11
  285.2 12.5 %select_subtract_fusion.2 = f32[4096,1024]{1,0:T(8,128)} fusion(f32[4096,1024]{1,0:T(8,128)} %select_dynamic-update-slice_fusion.2, bf16[4096,256]{1,0:T(8,128)(2,1)} %all-reduce.3.cloned.1.call-done, bf16[256,1024]{1,0:T(8,128)(2,1)} %all-reduce.5.cloned.1.call-done, pred[4096]{0:T(1024)(128)(4,1)S(1)} %fusion.40), kind=kOutput, calls=%fused_computation.3.clone.1 | convolution fusion | flops 2155872256 | bytes 36179968 | tf_op jit(solution)/shard_map/while/body/eval_jaxpr/dot_general | solution.py:47
  297.7 3.3 dynamic-slice_select_fusion.2
  301.1 51.4 %all-reduce.3.cloned.1.call-done = bf16[4096,256]{1,0:T(8,128)(2,1)} async-done(((bf16[4096,256]{1,0:T(8,128)(2,1)}), bf16[4096,256]{1,0:T(8,128)(2,1)}) %all-reduce.3.cloned.1.call-update) | async-done | bytes 2097168 | tf_op jit(solution)/shard_map/while/body/eval_jaxpr/psum | solution.py:11
  353.5 3.9 while.24
  357.4 19.7 %custom-call.17 = f32[2,128,128]{1,2,0:T(8,128)S(1)} custom-call(f32[2,128,128]{2,1,0:T(8,128)S(1)} %get-tuple-element.282), custom_call_target="InvertDiagBlocksLowerTriangular" | custom-call | tf_op jit(solution)/shard_map/while/body/eval_jaxpr/triangular_solve | solution.py:36
  382.0 2.3 select_dynamic-update-slice_fusion.2
  384.4 36.2 %all-reduce.5.cloned.1.call-done = bf16[256,1024]{1,0:T(8,128)(2,1)} async-done(((bf16[256,1024]{1,0:T(8,128)(2,1)}), bf16[256,1024]{1,0:T(8,128)(2,1)}) %all-reduce.5.cloned.1.call-update) | async-done | bytes 524304 | tf_op jit(solution)/shard_map/while/body/eval_jaxpr/psum | solution.py:11
  420.6 12.5 %select_subtract_fusion.2 = f32[4096,1024]{1,0:T(8,128)} fusion(f32[4096,1024]{1,0:T(8,128)} %select_dynamic-update-slice_fusion.2, bf16[4096,256]{1,0:T(8,128)(2,1)} %all-reduce.3.cloned.1.call-done, bf16[256,1024]{1,0:T(8,128)(2,1)} %all-reduce.5.cloned.1.call-done, pred[4096]{0:T(1024)(128)(4,1)S(1)} %fusion.40), kind=kOutput, calls=%fused_computation.3.clone.1 | convolution fusion | flops 2155872256 | bytes 36179968 | tf_op jit(solution)/shard_map/while/body/eval_jaxpr/dot_general | solution.py:47
  433.1 3.3 dynamic-slice_select_fusion.2
  436.5 51.4 %all-reduce.3.cloned.1.call-done = bf16[4096,256]{1,0:T(8,128)(2,1)} async-done(((bf16[4096,256]{1,0:T(8,128)(2,1)}), bf16[4096,256]{1,0:T(8,128)(2,1)}) %all-reduce.3.cloned.1.call-update) | async-done | bytes 2097168 | tf_op jit(solution)/shard_map/while/body/eval_jaxpr/psum | solution.py:11
  488.9 3.9 while.24
  492.8 19.7 %custom-call.17 = f32[2,128,128]{1,2,0:T(8,128)S(1)} custom-call(f32[2,128,128]{2,1,0:T(8,128)S(1)} %get-tuple-element.282), custom_call_target="InvertDiagBlocksLowerTriangular" | custom-call | tf_op jit(solution)/shard_map/while/body/eval_jaxpr/triangular_solve | solution.py:36
  512.5 1.7 fusion.37
  517.4 2.3 select_dynamic-update-slice_fusion.2
  519.8 36.2 %all-reduce.5.cloned.1.call-done = bf16[256,1024]{1,0:T(8,128)(2,1)} async-done(((bf16[256,1024]{1,0:T(8,128)(2,1)}), bf16[256,1024]{1,0:T(8,128)(2,1)}) %all-reduce.5.cloned.1.call-update) | async-done | bytes 524304 | tf_op jit(solution)/shard_map/while/body/eval_jaxpr/psum | solution.py:11
  556.0 12.5 %select_subtract_fusion.2 = f32[4096,1024]{1,0:T(8,128)} fusion(f32[4096,1024]{1,0:T(8,128)} %select_dynamic-update-slice_fusion.2, bf16[4096,256]{1,0:T(8,128)(2,1)} %all-reduce.3.cloned.1.call-done, bf16[256,1024]{1,0:T(8,128)(2,1)} %all-reduce.5.cloned.1.call-done, pred[4096]{0:T(1024)(128)(4,1)S(1)} %fusion.40), kind=kOutput, calls=%fused_computation.3.clone.1 | convolution fusion | flops 2155872256 | bytes 36179968 | tf_op jit(solution)/shard_map/while/body/eval_jaxpr/dot_general | solution.py:47
  568.5 3.3 dynamic-slice_select_fusion.2
  571.9 51.4 %all-reduce.3.cloned.1.call-done = bf16[4096,256]{1,0:T(8,128)(2,1)} async-done(((bf16[4096,256]{1,0:T(8,128)(2,1)}), bf16[4096,256]{1,0:T(8,128)(2,1)}) %all-reduce.3.cloned.1.call-update) | async-done | bytes 2097168 | tf_op jit(solution)/shard_map/while/body/eval_jaxpr/psum | solution.py:11
  624.3 3.9 while.24
  628.2 19.7 %custom-call.17 = f32[2,128,128]{1,2,0:T(8,128)S(1)} custom-call(f32[2,128,128]{2,1,0:T(8,128)S(1)} %get-tuple-element.282), custom_call_target="InvertDiagBlocksLowerTriangular" | custom-call | tf_op jit(solution)/shard_map/while/body/eval_jaxpr/triangular_solve | solution.py:36
  647.9 1.7 fusion.37
  652.8 2.3 select_dynamic-update-slice_fusion.2
  655.2 36.2 %all-reduce.5.cloned.1.call-done = bf16[256,1024]{1,0:T(8,128)(2,1)} async-done(((bf16[256,1024]{1,0:T(8,128)(2,1)}), bf16[256,1024]{1,0:T(8,128)(2,1)}) %all-reduce.5.cloned.1.call-update) | async-done | bytes 524304 | tf_op jit(solution)/shard_map/while/body/eval_jaxpr/psum | solution.py:11
  691.4 12.5 %select_subtract_fusion.2 = f32[4096,1024]{1,0:T(8,128)} fusion(f32[4096,1024]{1,0:T(8,128)} %select_dynamic-update-slice_fusion.2, bf16[4096,256]{1,0:T(8,128)(2,1)} %all-reduce.3.cloned.1.call-done, bf16[256,1024]{1,0:T(8,128)(2,1)} %all-reduce.5.cloned.1.call-done, pred[4096]{0:T(1024)(128)(4,1)S(1)} %fusion.40), kind=kOutput, calls=%fused_computation.3.clone.1 | convolution fusion | flops 2155872256 | bytes 36179968 | tf_op jit(solution)/shard_map/while/body/eval_jaxpr/dot_general | solution.py:47
  703.9 3.3 dynamic-slice_select_fusion.2
  707.3 51.4 %all-reduce.3.cloned.1.call-done = bf16[4096,256]{1,0:T(8,128)(2,1)} async-done(((bf16[4096,256]{1,0:T(8,128)(2,1)}), bf16[4096,256]{1,0:T(8,128)(2,1)}) %all-reduce.3.cloned.1.call-update) | async-done | bytes 2097168 | tf_op jit(solution)/shard_map/while/body/eval_jaxpr/psum | solution.py:11
  759.7 3.9 while.24
  763.6 19.7 %custom-call.17 = f32[2,128,128]{1,2,0:T(8,128)S(1)} custom-call(f32[2,128,128]{2,1,0:T(8,128)S(1)} %get-tuple-element.282), custom_call_target="InvertDiagBlocksLowerTriangular" | custom-call | tf_op jit(solution)/shard_map/while/body/eval_jaxpr/triangular_solve | solution.py:36
  788.2 2.3 select_dynamic-update-slice_fusion.2
  790.6 36.2 %all-reduce.5.cloned.1.call-done = bf16[256,1024]{1,0:T(8,128)(2,1)} async-done(((bf16[256,1024]{1,0:T(8,128)(2,1)}), bf16[256,1024]{1,0:T(8,128)(2,1)}) %all-reduce.5.cloned.1.call-update) | async-done | bytes 524304 | tf_op jit(solution)/shard_map/while/body/eval_jaxpr/psum | solution.py:11
  826.8 12.5 %select_subtract_fusion.2 = f32[4096,1024]{1,0:T(8,128)} fusion(f32[4096,1024]{1,0:T(8,128)} %select_dynamic-update-slice_fusion.2, bf16[4096,256]{1,0:T(8,128)(2,1)} %all-reduce.3.cloned.1.call-done, bf16[256,1024]{1,0:T(8,128)(2,1)} %all-reduce.5.cloned.1.call-done, pred[4096]{0:T(1024)(128)(4,1)S(1)} %fusion.40), kind=kOutput, calls=%fused_computation.3.clone.1 | convolution fusion | flops 2155872256 | bytes 36179968 | tf_op jit(solution)/shard_map/while/body/eval_jaxpr/dot_general | solution.py:47
  839.2 3.3 dynamic-slice_select_fusion.2
  842.7 51.4 %all-reduce.3.cloned.1.call-done = bf16[4096,256]{1,0:T(8,128)(2,1)} async-done(((bf16[4096,256]{1,0:T(8,128)(2,1)}), bf16[4096,256]{1,0:T(8,128)(2,1)}) %all-reduce.3.cloned.1.call-update) | async-done | bytes 2097168 | tf_op jit(solution)/shard_map/while/body/eval_jaxpr/psum | solution.py:11
  895.1 3.9 while.24
  899.0 19.7 %custom-call.17 = f32[2,128,128]{1,2,0:T(8,128)S(1)} custom-call(f32[2,128,128]{2,1,0:T(8,128)S(1)} %get-tuple-element.282), custom_call_target="InvertDiagBlocksLowerTriangular" | custom-call | tf_op jit(solution)/shard_map/while/body/eval_jaxpr/triangular_solve | solution.py:36
  918.7 1.7 fusion.37
  923.6 2.3 select_dynamic-update-slice_fusion.2
  926.0 36.2 %all-reduce.5.cloned.1.call-done = bf16[256,1024]{1,0:T(8,128)(2,1)} async-done(((bf16[256,1024]{1,0:T(8,128)(2,1)}), bf16[256,1024]{1,0:T(8,128)(2,1)}) %all-reduce.5.cloned.1.call-update) | async-done | bytes 524304 | tf_op jit(solution)/shard_map/while/body/eval_jaxpr/psum | solution.py:11
  962.1 12.5 %select_subtract_fusion.2 = f32[4096,1024]{1,0:T(8,128)} fusion(f32[4096,1024]{1,0:T(8,128)} %select_dynamic-update-slice_fusion.2, bf16[4096,256]{1,0:T(8,128)(2,1)} %all-reduce.3.cloned.1.call-done, bf16[256,1024]{1,0:T(8,128)(2,1)} %all-reduce.5.cloned.1.call-done, pred[4096]{0:T(1024)(128)(4,1)S(1)} %fusion.40), kind=kOutput, calls=%fused_computation.3.clone.1 | convolution fusion | flops 2155872256 | bytes 36179968 | tf_op jit(solution)/shard_map/while/body/eval_jaxpr/dot_general | solution.py:47
  974.6 3.3 dynamic-slice_select_fusion.2
  978.1 51.4 %all-reduce.3.cloned.1.call-done = bf16[4096,256]{1,0:T(8,128)(2,1)} async-done(((bf16[4096,256]{1,0:T(8,128)(2,1)}), bf16[4096,256]{1,0:T(8,128)(2,1)}) %all-reduce.3.cloned.1.call-update) | async-done | bytes 2097168 | tf_op jit(solution)/shard_map/while/body/eval_jaxpr/psum | solution.py:11
  1030.5 3.9 while.24
  1034.4 19.7 %custom-call.17 = f32[2,128,128]{1,2,0:T(8,128)S(1)} custom-call(f32[2,128,128]{2,1,0:T(8,128)S(1)} %get-tuple-element.282), custom_call_target="InvertDiagBlocksLowerTriangular" | custom-call | tf_op jit(solution)/shard_map/while/body/eval_jaxpr/triangular_solve | solution.py:36
  1059.0 2.3 select_dynamic-update-slice_fusion.2
  1061.4 36.2 %all-reduce.5.cloned.1.call-done = bf16[256,1024]{1,0:T(8,128)(2,1)} async-done(((bf16[256,1024]{1,0:T(8,128)(2,1)}), bf16[256,1024]{1,0:T(8,128)(2,1)}) %all-reduce.5.cloned.1.call-update) | async-done | bytes 524304 | tf_op jit(solution)/shard_map/while/body/eval_jaxpr/psum | solution.py:11
  1097.5 12.5 %select_subtract_fusion.2 = f32[4096,1024]{1,0:T(8,128)} fusion(f32[4096,1024]{1,0:T(8,128)} %select_dynamic-update-slice_fusion.2, bf16[4096,256]{1,0:T(8,128)(2,1)} %all-reduce.3.cloned.1.call-done, bf16[256,1024]{1,0:T(8,128)(2,1)} %all-reduce.5.cloned.1.call-done, pred[4096]{0:T(1024)(128)(4,1)S(1)} %fusion.40), kind=kOutput, calls=%fused_computation.3.clone.1 | convolution fusion | flops 2155872256 | bytes 36179968 | tf_op jit(solution)/shard_map/while/body/eval_jaxpr/dot_general | solution.py:47
  (147 shorter events, 70.4 us)
Async XLA Ops:
  24.1 57.6 %all-reduce.3.cloned.1.call-start = ((), (), s32[]{:S(2)}) async-start(), calls=%async_computation | async-start | bytes 4194304 | tf_op jit(solution)/shard_map/while/body/eval_jaxpr/psum | solution.py:11
  27.5 122.3 %all-reduce.5.cloned.1.call-start = ((), (), s32[]{:S(2)}) async-start(), calls=%async_computation.1 | async-start | bytes 1048576 | tf_op jit(solution)/shard_map/while/body/eval_jaxpr/psum | solution.py:11
  162.3 54.8 %all-reduce.3.cloned.1.call-start = ((), (), s32[]{:S(2)}) async-start(), calls=%async_computation | async-start | bytes 4194304 | tf_op jit(solution)/shard_map/while/body/eval_jaxpr/psum | solution.py:11
  165.6 119.6 %all-reduce.5.cloned.1.call-start = ((), (), s32[]{:S(2)}) async-start(), calls=%async_computation.1 | async-start | bytes 1048576 | tf_op jit(solution)/shard_map/while/body/eval_jaxpr/psum | solution.py:11
  297.7 54.8 %all-reduce.3.cloned.1.call-start = ((), (), s32[]{:S(2)}) async-start(), calls=%async_computation | async-start | bytes 4194304 | tf_op jit(solution)/shard_map/while/body/eval_jaxpr/psum | solution.py:11
  301.0 119.6 %all-reduce.5.cloned.1.call-start = ((), (), s32[]{:S(2)}) async-start(), calls=%async_computation.1 | async-start | bytes 1048576 | tf_op jit(solution)/shard_map/while/body/eval_jaxpr/psum | solution.py:11
  433.0 54.8 %all-reduce.3.cloned.1.call-start = ((), (), s32[]{:S(2)}) async-start(), calls=%async_computation | async-start | bytes 4194304 | tf_op jit(solution)/shard_map/while/body/eval_jaxpr/psum | solution.py:11
  436.4 119.6 %all-reduce.5.cloned.1.call-start = ((), (), s32[]{:S(2)}) async-start(), calls=%async_computation.1 | async-start | bytes 1048576 | tf_op jit(solution)/shard_map/while/body/eval_jaxpr/psum | solution.py:11
  568.4 54.8 %all-reduce.3.cloned.1.call-start = ((), (), s32[]{:S(2)}) async-start(), calls=%async_computation | async-start | bytes 4194304 | tf_op jit(solution)/shard_map/while/body/eval_jaxpr/psum | solution.py:11
  571.8 119.6 %all-reduce.5.cloned.1.call-start = ((), (), s32[]{:S(2)}) async-start(), calls=%async_computation.1 | async-start | bytes 1048576 | tf_op jit(solution)/shard_map/while/body/eval_jaxpr/psum | solution.py:11
  703.8 54.8 %all-reduce.3.cloned.1.call-start = ((), (), s32[]{:S(2)}) async-start(), calls=%async_computation | async-start | bytes 4194304 | tf_op jit(solution)/shard_map/while/body/eval_jaxpr/psum | solution.py:11
  707.2 119.6 %all-reduce.5.cloned.1.call-start = ((), (), s32[]{:S(2)}) async-start(), calls=%async_computation.1 | async-start | bytes 1048576 | tf_op jit(solution)/shard_map/while/body/eval_jaxpr/psum | solution.py:11
  839.2 54.8 %all-reduce.3.cloned.1.call-start = ((), (), s32[]{:S(2)}) async-start(), calls=%async_computation | async-start | bytes 4194304 | tf_op jit(solution)/shard_map/while/body/eval_jaxpr/psum | solution.py:11
  842.6 119.6 %all-reduce.5.cloned.1.call-start = ((), (), s32[]{:S(2)}) async-start(), calls=%async_computation.1 | async-start | bytes 1048576 | tf_op jit(solution)/shard_map/while/body/eval_jaxpr/psum | solution.py:11
  974.6 54.8 %all-reduce.3.cloned.1.call-start = ((), (), s32[]{:S(2)}) async-start(), calls=%async_computation | async-start | bytes 4194304 | tf_op jit(solution)/shard_map/while/body/eval_jaxpr/psum | solution.py:11
  978.0 119.6 %all-reduce.5.cloned.1.call-start = ((), (), s32[]{:S(2)}) async-start(), calls=%async_computation.1 | async-start | bytes 1048576 | tf_op jit(solution)/shard_map/while/body/eval_jaxpr/psum | solution.py:11
Sparse Core Ops, SparseCore 0:
  27.6 54.0 all-reduce.2
  111.3 38.3 all-reduce.4
  165.7 51.3 all-reduce.2
  246.7 38.3 all-reduce.4
  301.1 51.3 all-reduce.2
  382.1 38.3 all-reduce.4
  436.5 51.3 all-reduce.2
  517.5 38.3 all-reduce.4
  571.9 51.3 all-reduce.2
  652.9 38.3 all-reduce.4
  707.3 51.3 all-reduce.2
  788.3 38.3 all-reduce.4
  842.7 51.3 all-reduce.2
  923.7 38.3 all-reduce.4
  978.1 51.3 all-reduce.2
  1059.1 38.3 all-reduce.4
where the time goes:
time: 1120 us
  waiting for transfers between devices  704 us (63%)
  other arithmetic  235 us (21%)
  matrix products  131 us (12%)
  local copies, waits for them, and re-layouts  31.7 us (3%)
  between operations  13.1 us (1%)
    psum x16, waiting for transfers between devices, broadcast(): return lax.psum(jnp.where(mine, shard, jnp.zeros_like(shard)), axis)  703 us
    another operation x24, other arithmetic, solve_at(): lax.linalg.triangular_solve(diagonal, right_side, left_side=True, lower=T...  165 us
    dot_general x8, matrix products, apply_block(): jnp.dot(column_tile, sent_block, preferred_element_type=jnp.float32)  100 us
    select_n x16, other arithmetic, broadcast(): return lax.psum(jnp.where(mine, shard, jnp.zeros_like(shard)), axis)  33.7 us
    another operation x24, matrix products, solve_at(): lax.linalg.triangular_solve(diagonal, right_side, left_side=True, lower=T...  31.5 us
    another operation x48, local copies, waits for them, and re-layouts  31.2 us
  transfers between devices with their start and end apart: 16, of which 16 were waited for; matrix products, arithmetic and copies ran while one was open for 2% of the time, Pallas kernels for 0%

commit v1 on v0

--- a/solution.py
+++ b/solution.py
@@ -1,17 +1,26 @@
+import functools
+
 import jax
 import jax.numpy as jnp
 from jax import lax
+from jax.experimental import pallas as pl
+from jax.experimental.pallas import tpu as pltpu
 from jax.sharding import PartitionSpec as P
 
 STEPS = 8
-
+ROWS = 4
+COLS = 4
+SPLIT = 4
+HALF = 128
+GROUP = 2
+MESH = pl.DeviceIdType.MESH
 
 def broadcast(shard, axis, root):
     mine = lax.axis_index(axis) == root
     return lax.psum(jnp.where(mine, shard, jnp.zeros_like(shard)), axis)
 
 
-def local(factor, gradient):
+def general(factor, gradient):
     row_count = lax.axis_size("row")
     my_row = lax.axis_index("row")
     cycles, _, block_size, width_local = factor.shape
@@ -56,6 +65,334 @@
 
     current = lax.fori_loop(0, STEPS, advance, current)
     return current.reshape(gradient.shape)
+
+
+def exact_dot(a, b):
+    return jnp.dot(a, b, precision=lax.Precision.HIGHEST, preferred_element_type=jnp.float32)
+
+
+def invert_lower(lower):
+    size = lower.shape[0]
+    row = lax.broadcasted_iota(jnp.int32, (size, size), 0)
+    col = lax.broadcasted_iota(jnp.int32, (size, size), 1)
+    diagonal = jnp.where(row == col, lower, 0.0)
+    scale_col = 1.0 / jnp.sum(diagonal, axis=0, keepdims=True)
+    scale_row = 1.0 / jnp.sum(diagonal, axis=1, keepdims=True)
+    pair = (row == col + 1) & (row % 2 == 1)
+    inverse = jnp.where(row == col, scale_row, 0.0) - jnp.where(
+        pair, scale_row * lower * scale_col, 0.0
+    )
+    width = 2
+    while width < size:
+        below = (
+            (row // (2 * width) == col // (2 * width))
+            & ((row // width) % 2 == 1)
+            & ((col // width) % 2 == 0)
+        )
+        step = exact_dot(jnp.where(below, lower, 0.0), inverse)
+        inverse = inverse - exact_dot(inverse, step)
+        width *= 2
+    return inverse
+
+
+def solve_kernel(
+    panel, grad, gathered, every_solved, own_solved,
+    top, solved, inverse,
+    x_send, x_recv, s_send, s_recv, f_send, f_recv,
+    up_send, down_send, z_recv, local_sem,
+):
+    col = lax.axis_index("col")
+    row = lax.axis_index("row")
+    block = top.shape[2]
+    chunk = solved.shape[2]
+    heads = top.shape[1]
+    groups = gathered.shape[1] // GROUP
+    partner = (col + 2) % COLS
+    sibling = col + 1 - 2 * (col % 2)
+
+    barrier = pltpu.get_barrier_semaphore()
+    for other in (partner, sibling):
+        pl.semaphore_signal(barrier, inc=1, device_id={"col": other}, device_id_type=MESH)
+
+    @pl.when(row > 0)
+    def _():
+        pl.semaphore_signal(barrier, inc=1, device_id={"row": row - 1}, device_id_type=MESH)
+
+    @pl.when(row < ROWS - 1)
+    def _():
+        pl.semaphore_signal(barrier, inc=1, device_id={"row": row + 1}, device_id_type=MESH)
+
+    inner = (row > 0) & (row < ROWS - 1)
+
+    @pl.when(inner)
+    def _():
+        pl.semaphore_wait(barrier, 4)
+
+    @pl.when(jnp.logical_not(inner))
+    def _():
+        pl.semaphore_wait(barrier, 3)
+
+    def place(slab, item):
+        if isinstance(item, int) and item < heads:
+            return top.at[slab, item]
+        return gathered.at[slab, pl.ds((item - heads) * GROUP, GROUP)]
+
+    def source(item):
+        if isinstance(item, int) and item < heads:
+            return panel.at[item]
+        return panel.at[pl.ds(heads + (item - heads) * GROUP, GROUP)]
+
+    def to_partner(item):
+        return pltpu.make_async_remote_copy(
+            src_ref=source(item), dst_ref=place(col, item),
+            send_sem=x_send.at[item], recv_sem=x_recv.at[item],
+            device_id={"col": partner}, device_id_type=MESH,
+        )
+
+    def to_sibling(item):
+        return pltpu.make_async_remote_copy(
+            src_ref=source(item), dst_ref=place(col, item),
+            send_sem=s_send.at[item], recv_sem=s_recv.at[item],
+            device_id={"col": sibling}, device_id_type=MESH,
+        )
+
+    def forward(item):
+        return pltpu.make_async_remote_copy(
+            src_ref=place(partner, item), dst_ref=place(partner, item),
+            send_sem=f_send.at[item], recv_sem=f_recv.at[item],
+            device_id={"col": sibling}, device_id_type=MESH,
+        )
+
+    def pass_on(item):
+        to_partner(item).wait_recv()
+        forward(item).start()
+
+    def keep_head(item):
+        return pltpu.make_async_copy(panel.at[item], top.at[col, item], local_sem.at[item])
+
+    keep_rest = pltpu.make_async_copy(
+        panel.at[pl.ds(heads, groups * GROUP)], gathered.at[col], local_sem.at[heads]
+    )
+
+    for item in range(heads):
+        to_partner(item).start()
+        to_sibling(item).start()
+        keep_head(item).start()
+
+    def receive_head(item):
+        keep_head(item).wait()
+        pass_on(item)
+        to_sibling(item).wait_recv()
+        forward(item).wait_recv()
+
+    def invert(index):
+        slab = row // 2 + 2 * index
+        for half in range(2):
+            start = pl.multiple_of((row % 2) * block + half * HALF, HALF)
+            diagonal = top[slab, index, half * HALF:(half + 1) * HALF, pl.ds(start, HALF)]
+            inverse[index, half] = invert_lower(diagonal.astype(jnp.float32))
+
+    receive_head(0)
+
+    @pl.loop(heads, heads + groups)
+    def _(item):
+        to_partner(item).start()
+
+    invert(0)
+    receive_head(1)
+
+    @pl.when(row > 0)
+    def _():
+        invert(1)
+
+    @pl.loop(heads, heads + groups)
+    def _(item):
+        to_sibling(item).start()
+
+    keep_rest.start()
+
+    def send_row(position, part, step, sems):
+        piece = solved.at[part, pl.ds(position * block, block)]
+        return pltpu.make_async_remote_copy(
+            src_ref=piece, dst_ref=piece,
+            send_sem=sems.at[position * SPLIT + part],
+            recv_sem=z_recv.at[position * SPLIT + part],
+            device_id={"row": row + step}, device_id_type=MESH,
+        )
+
+    def solve(position, part):
+        index = position // ROWS
+        columns = pl.ds(pl.multiple_of(part * chunk, chunk), chunk)
+        right = grad[index, :, columns].astype(jnp.float32)
+        width = top.shape[3]
+        done = 0
+        while done < position * block:
+            take = min(width, position * block - done)
+            right = right - jnp.dot(
+                top[done // width, index, :, 0:take],
+                solved[part, done:done + take, :],
+                preferred_element_type=jnp.float32,
+            )
+            done += take
+        first = exact_dot(inverse[index, 0], right[:HALF])
+        slab, start = position * block // width, position * block % width
+        below = top[slab, index, HALF:, start:start + HALF].astype(jnp.float32)
+        second = exact_dot(inverse[index, 1], right[HALF:] - exact_dot(below, first))
+        own_solved[index, :HALF, columns] = first
+        own_solved[index, HALF:, columns] = second
+        base = position * block
+        solved[part, base:base + HALF, :] = first.astype(jnp.bfloat16)
+        solved[part, base + HALF:base + block, :] = second.astype(jnp.bfloat16)
+
+    def for_sends(position, part, act):
+        owner = position % ROWS
+
+        @pl.when((row >= owner) & (row < ROWS - 1))
+        def _():
+            act(send_row(position, part, 1, up_send))
+
+        @pl.when((row <= owner) & (row > 0))
+        def _():
+            act(send_row(position, part, -1, down_send))
+
+    @pl.loop(0, STEPS + SPLIT - 1)
+    def _(wave):
+        for position in range(STEPS):
+            part = wave - position
+
+            @pl.when((part >= 0) & (part < SPLIT))
+            def _():
+                @pl.when(row == position % ROWS)
+                def _():
+                    solve(position, part)
+
+                @pl.when(row != position % ROWS)
+                def _():
+                    send_row(position, part, 0, up_send).wait_recv()
+
+                for_sends(position, part, lambda copy: copy.start())
+
+        @pl.when((wave == ROWS - 1) & (row == 0))
+        def _():
+            invert(1)
+
+        @pl.when((wave % 2 == 1) & (wave // 2 < groups))
+        def _():
+            pass_on(heads + wave // 2)
+
+    passed = min(groups, (STEPS + SPLIT - 1) // 2)
+
+    write_solved = pltpu.make_async_copy(solved, every_solved, local_sem.at[heads + 1])
+    write_solved.start()
+
+    @pl.loop(heads + passed, heads + groups)
+    def _(item):
+        pass_on(item)
+
+    for item in range(heads):
+        to_partner(item).wait_send()
+        to_sibling(item).wait_send()
+        forward(item).wait_send()
+
+    @pl.loop(heads, heads + groups)
+    def _(item):
+        to_partner(item).wait_send()
+        to_sibling(item).wait()
+        forward(item).wait()
+
+    for position in range(STEPS):
+        @pl.loop(0, SPLIT)
+        def _(part):
+            for_sends(position, part, lambda copy: copy.wait_send())
+
+    keep_rest.wait()
+    write_solved.wait()
+
+
+def trailing_kernel(heads, gathered, every_solved, own_solved, grad, out):
+    cycle = pl.program_id(0)
+
+    @pl.when(cycle < heads)
+    def _():
+        out[0] = own_solved[0]
+
+    @pl.when(cycle >= heads)
+    def _():
+        chunk = every_solved.shape[2]
+        width = gathered.shape[3]
+        for part in range(every_solved.shape[0]):
+            columns = slice(part * chunk, (part + 1) * chunk)
+            total = grad[0, :, columns].astype(jnp.float32)
+            for slab in range(gathered.shape[0]):
+                total = total - jnp.dot(
+                    gathered[slab, 0],
+                    every_solved[part, slab * width:(slab + 1) * width, :],
+                    preferred_element_type=jnp.float32,
+                )
+            out[0, :, columns] = total
+
+
+def fused(factor, gradient):
+    cycles, _, block, width = factor.shape
+    columns = gradient.shape[3]
+    heads = STEPS // ROWS
+    chunk = columns // SPLIT
+    items = heads + (cycles - heads) // GROUP
+    panel = factor.reshape(cycles, block, width).astype(jnp.bfloat16)
+    grad = gradient.reshape(cycles, block, columns)
+    dma = pltpu.SemaphoreType.DMA
+    any_spec = pl.BlockSpec(memory_space=pl.ANY)
+    vmem_spec = pl.BlockSpec(memory_space=pltpu.VMEM)
+    gathered, every_solved, own_solved = pl.pallas_call(
+        solve_kernel,
+        out_shape=(
+            jax.ShapeDtypeStruct((COLS, cycles - heads, block, width), jnp.bfloat16),
+            jax.ShapeDtypeStruct((SPLIT, STEPS * block, chunk), jnp.bfloat16),
+            jax.ShapeDtypeStruct((heads, block, columns), jnp.float32),
+        ),
+        in_specs=[any_spec, vmem_spec],
+        out_specs=(any_spec, any_spec, vmem_spec),
+        scratch_shapes=[
+            pltpu.VMEM((COLS, heads, block, width), jnp.bfloat16),
+            pltpu.VMEM((SPLIT, STEPS * block, chunk), jnp.bfloat16),
+            pltpu.VMEM((heads, 2, HALF, HALF), jnp.float32),
+        ]
+        + [dma((items,))] * 6
+        + [dma((STEPS * SPLIT,))] * 3
+        + [dma((heads + 2,))],
+        compiler_params=pltpu.CompilerParams(
+            collective_id=0, has_side_effects=True, vmem_limit_bytes=56 * 1024 * 1024
+        ),
+    )(panel, grad[:heads])
+    out = pl.pallas_call(
+        functools.partial(trailing_kernel, heads),
+        grid=(cycles,),
+        out_shape=jax.ShapeDtypeStruct((cycles, block, columns), jnp.float32),
+        in_specs=[
+            pl.BlockSpec((COLS, 1, block, width), lambda i: (0, jnp.maximum(i - heads, 0), 0, 0)),
+            pl.BlockSpec((SPLIT, STEPS * block, chunk), lambda i: (0, 0, 0)),
+            pl.BlockSpec((1, block, columns), lambda i: (jnp.minimum(i, heads - 1), 0, 0)),
+            pl.BlockSpec((1, block, columns), lambda i: (i, 0, 0)),
+        ],
+        out_specs=pl.BlockSpec((1, block, columns), lambda i: (i, 0, 0)),
+        compiler_params=pltpu.CompilerParams(
+            dimension_semantics=("arbitrary",), vmem_limit_bytes=56 * 1024 * 1024
+        ),
+    )(gathered, every_solved, own_solved, grad)
+    return out.reshape(gradient.shape)
+
+
+def local(factor, gradient):
+    cycles, _, block, width = factor.shape
+    fits = (
+        lax.axis_size("row") == ROWS
+        and lax.axis_size("col") == COLS
+        and width == 2 * block
+        and block == 2 * HALF
+        and COLS * width == STEPS * block
+        and (cycles - STEPS // ROWS) % GROUP == 0
+    )
+    return fused(factor, gradient) if fits else general(factor, gradient)
 
 
 def solution(mesh):

time: 1120 us -> 288 us (0.26)
  waiting for transfers between devices: 704 us -> 0 us
  Pallas kernels: 0 us -> 279 us
  other arithmetic: 235 us -> 5.97 us
  matrix products: 131 us -> 0 us
  local copies, waits for them, and re-layouts: 31.7 us -> 2.26 us
  between operations: 13.1 us -> 0.01 us
    psum x16 -> x0, waiting for transfers between devices: 703 us -> none  [broadcast(): return lax.psum(jnp.where(mine, shard, jnp.zeros_like(shard)), axis)]
    pallas_call x0 -> x2, Pallas kernels: none -> 279 us  [the longest x1 253 us: fused(): pl.pallas_call(solve_kernel, out_shape=(jax.ShapeDtypeStruct((COLS, cycle...]
    another operation x24 -> x0, other arithmetic: 165 us -> none  [solve_at(): lax.linalg.triangular_solve(diagonal, right_side, left_side=True, lower=T...]
    dot_general x8 -> x0, matrix products: 100 us -> none  [apply_block(): jnp.dot(column_tile, sent_block, preferred_element_type=jnp.float32)]
    select_n x24 -> x0, other arithmetic: 52.4 us -> none  [the longest x16 33.7 us: broadcast(): return lax.psum(jnp.where(mine, shard, jnp.zeros_like(shard)), axis)]
    another operation x56 -> x0, local copies, waits for them, and re-layouts: 31.7 us -> none
    another operation x24 -> x0, matrix products: 31.5 us -> none  [solve_at(): lax.linalg.triangular_solve(diagonal, right_side, left_side=True, lower=T...]
    convert_element_type x2 -> x1, other arithmetic: 17.6 us -> 5.97 us  [fused(): panel = factor.reshape(cycles, block, width).astype(jnp.bfloat16)]
  transfers between devices with their start and end apart: 16 -> 0, of which waited for: 16 -> 0; matrix products, arithmetic and copies ran while one was open for 2% -> 0% of each run, Pallas kernels for 0% -> 0%
where the time goes in v1:
time: 288 us
  Pallas kernels  279 us (97%)
  other arithmetic  5.97 us (2%)
    pallas_call x1, Pallas kernels, fused(): pl.pallas_call(solve_kernel, out_shape=(jax.ShapeDtypeStruct((COLS, cycle...  253 us
    pallas_call x1, Pallas kernels, fused(): pl.pallas_call(functools.partial(trailing_kernel, heads), grid=(cycles,),...  26.8 us
    convert_element_type x1, other arithmetic, fused(): panel = factor.reshape(cycles, block, width).astype(jnp.bfloat16)  5.97 us

profile of v1, /device:TPU:0, one launch (start us, length us, event | category | flops | bytes accessed | tf_op | source)
XLA Modules:
  0.0 287.7 jit_solution(16693484444253075516)
XLA Ops:
  0.0 2.3 slice_bitcast_fusion.grad
  2.3 6.0 %fusion.panel = bf16[16,256,512]{2,1,0:T(8,128)(2,1)} fusion(f32[16,1,256,512]{3,2,1,0:T(8,128)} %param.2), kind=kLoop, calls=%fused_computation.1 | loop fusion | flops 2097152 | bytes 12582912 | tf_op jit(solution)/shard_map/convert_element_type | solution.py:341
  8.2 252.7 %shard_map.28 = (bf16[4,14,256,512]{3,2,1,0:T(8,128)(2,1)}, bf16[4,2048,256]{2,1,0:T(8,128)(2,1)}, f32[2,256,1024]{2,1,0:T(8,128)}) custom-call(bf16[16,256,512]{2,1,0:T(8,128)(2,1)} %fusion.panel, bf16[2,256,1024]{2,1,0:T(8,128)(2,1)} %slice_bitcast_fusion.grad), custom_call_target="tpu_custom_call" | custom-call | tf_op jit(solution)/shard_map/pallas_call | solution.py:346
  260.9 26.8 %shard_map.29 = f32[16,256,1024]{2,1,0:T(8,128)} custom-call(bf16[4,14,256,512]{3,2,1,0:T(8,128)(2,1)} %get-tuple-element.8.gathered, bf16[4,2048,256]{2,1,0:T(8,128)(2,1)} %get-tuple-element.9.every_solved, f32[2,256,1024]{2,1,0:T(8,128)} %get-tuple-element.10.own_solved, bf16[16,256,1024]{2,1,0:T(8,128)(2,1)} %bitcast.14), custom_call_target="tpu_custom_call" | custom-call | tf_op jit(solution)/shard_map/pallas_call | solution.py:367

commit v2 on v1

--- a/solution.py
+++ b/solution.py
@@ -132,10 +132,10 @@
     def _():
         pl.semaphore_wait(barrier, 3)
 
-    def place(slab, item):
+    def place(slab, slot, item):
         if isinstance(item, int) and item < heads:
             return top.at[slab, item]
-        return gathered.at[slab, pl.ds((item - heads) * GROUP, GROUP)]
+        return gathered.at[slot, pl.ds((item - heads) * GROUP, GROUP)]
 
     def source(item):
         if isinstance(item, int) and item < heads:
@@ -144,21 +144,21 @@
 
     def to_partner(item):
         return pltpu.make_async_remote_copy(
-            src_ref=source(item), dst_ref=place(col, item),
+            src_ref=source(item), dst_ref=place(col, 0, item),
             send_sem=x_send.at[item], recv_sem=x_recv.at[item],
             device_id={"col": partner}, device_id_type=MESH,
         )
 
     def to_sibling(item):
         return pltpu.make_async_remote_copy(
-            src_ref=source(item), dst_ref=place(col, item),
+            src_ref=source(item), dst_ref=place(col, 1, item),
             send_sem=s_send.at[item], recv_sem=s_recv.at[item],
             device_id={"col": sibling}, device_id_type=MESH,
         )
 
     def forward(item):
         return pltpu.make_async_remote_copy(
-            src_ref=place(partner, item), dst_ref=place(partner, item),
+            src_ref=place(partner, 0, item), dst_ref=place(partner, 2, item),
             send_sem=f_send.at[item], recv_sem=f_recv.at[item],
             device_id={"col": sibling}, device_id_type=MESH,
         )
@@ -169,10 +169,6 @@
 
     def keep_head(item):
         return pltpu.make_async_copy(panel.at[item], top.at[col, item], local_sem.at[item])
-
-    keep_rest = pltpu.make_async_copy(
-        panel.at[pl.ds(heads, groups * GROUP)], gathered.at[col], local_sem.at[heads]
-    )
 
     for item in range(heads):
         to_partner(item).start()
@@ -208,8 +204,6 @@
     @pl.loop(heads, heads + groups)
     def _(item):
         to_sibling(item).start()
-
-    keep_rest.start()
 
     def send_row(position, part, step, sems):
         piece = solved.at[part, pl.ds(position * block, block)]
@@ -255,10 +249,17 @@
         def _():
             act(send_row(position, part, -1, down_send))
 
-    @pl.loop(0, STEPS + SPLIT - 1)
-    def _(wave):
+    starts = [0]
+    for position in range(1, STEPS):
+        hops = abs(position % ROWS - (position - 1) % ROWS)
+        starts.append(starts[-1] + 1 + hops)
+    ticks = starts[-1] + SPLIT + ROWS
+
+    @pl.loop(0, ticks)
+    def _(tick):
         for position in range(STEPS):
-            part = wave - position
+            hops = jnp.abs(row - position % ROWS)
+            part = tick - starts[position] - jnp.where(hops == 0, 0, 1 + hops)
 
             @pl.when((part >= 0) & (part < SPLIT))
             def _():
@@ -272,17 +273,17 @@
 
                 for_sends(position, part, lambda copy: copy.start())
 
-        @pl.when((wave == ROWS - 1) & (row == 0))
+        @pl.when((tick == SPLIT - 1) & (row == 0))
         def _():
             invert(1)
 
-        @pl.when((wave % 2 == 1) & (wave // 2 < groups))
+        @pl.when((tick % 3 == 2) & (tick // 3 < groups))
         def _():
-            pass_on(heads + wave // 2)
-
-    passed = min(groups, (STEPS + SPLIT - 1) // 2)
-
-    write_solved = pltpu.make_async_copy(solved, every_solved, local_sem.at[heads + 1])
+            pass_on(heads + tick // 3)
+
+    passed = min(groups, ticks // 3)
+
+    write_solved = pltpu.make_async_copy(solved, every_solved, local_sem.at[heads])
     write_solved.start()
 
     @pl.loop(heads + passed, heads + groups)
@@ -305,11 +306,11 @@
         def _(part):
             for_sends(position, part, lambda copy: copy.wait_send())
 
-    keep_rest.wait()
     write_solved.wait()
 
 
-def trailing_kernel(heads, gathered, every_solved, own_solved, grad, out):
+def trailing_kernel(heads, panel, gathered, every_solved, own_solved, grad, out):
+    col = lax.axis_index("col")
     cycle = pl.program_id(0)
 
     @pl.when(cycle < heads)
@@ -320,16 +321,20 @@
     def _():
         chunk = every_solved.shape[2]
         width = gathered.shape[3]
+        sibling = col + 1 - 2 * (col % 2)
+        slabs = (col, (col + 2) % COLS, sibling, (sibling + 2) % COLS)
+        lefts = (panel[0], gathered[0, 0], gathered[1, 0], gathered[2, 0])
         for part in range(every_solved.shape[0]):
             columns = slice(part * chunk, (part + 1) * chunk)
             total = grad[0, :, columns].astype(jnp.float32)
-            for slab in range(gathered.shape[0]):
-                total = total - jnp.dot(
-                    gathered[slab, 0],
-                    every_solved[part, slab * width:(slab + 1) * width, :],
+            product = jnp.zeros(total.shape, jnp.float32)
+            for left, slab in zip(lefts, slabs):
+                product = product + jnp.dot(
+                    left,
+                    every_solved[part, pl.ds(pl.multiple_of(slab * width, width), width), :],
                     preferred_element_type=jnp.float32,
                 )
-            out[0, :, columns] = total
+            out[0, :, columns] = total - product
 
 
 def fused(factor, gradient):
@@ -346,7 +351,7 @@
     gathered, every_solved, own_solved = pl.pallas_call(
         solve_kernel,
         out_shape=(
-            jax.ShapeDtypeStruct((COLS, cycles - heads, block, width), jnp.bfloat16),
+            jax.ShapeDtypeStruct((COLS - 1, cycles - heads, block, width), jnp.bfloat16),
             jax.ShapeDtypeStruct((SPLIT, STEPS * block, chunk), jnp.bfloat16),
             jax.ShapeDtypeStruct((heads, block, columns), jnp.float32),
         ),
@@ -359,7 +364,7 @@
         ]
         + [dma((items,))] * 6
         + [dma((STEPS * SPLIT,))] * 3
-        + [dma((heads + 2,))],
+        + [dma((heads + 1,))],
         compiler_params=pltpu.CompilerParams(
             collective_id=0, has_side_effects=True, vmem_limit_bytes=56 * 1024 * 1024
         ),
@@ -369,7 +374,8 @@
         grid=(cycles,),
         out_shape=jax.ShapeDtypeStruct((cycles, block, columns), jnp.float32),
         in_specs=[
-            pl.BlockSpec((COLS, 1, block, width), lambda i: (0, jnp.maximum(i - heads, 0), 0, 0)),
+            pl.BlockSpec((1, block, width), lambda i: (jnp.maximum(i, heads), 0, 0)),
+            pl.BlockSpec((COLS - 1, 1, block, width), lambda i: (0, jnp.maximum(i - heads, 0), 0, 0)),
             pl.BlockSpec((SPLIT, STEPS * block, chunk), lambda i: (0, 0, 0)),
             pl.BlockSpec((1, block, columns), lambda i: (jnp.minimum(i, heads - 1), 0, 0)),
             pl.BlockSpec((1, block, columns), lambda i: (i, 0, 0)),
@@ -378,7 +384,7 @@
         compiler_params=pltpu.CompilerParams(
             dimension_semantics=("arbitrary",), vmem_limit_bytes=56 * 1024 * 1024
         ),
-    )(gathered, every_solved, own_solved, grad)
+    )(panel, gathered, every_solved, own_solved, grad)
     return out.reshape(gradient.shape)
 
 

time: 288 us -> 170 us (0.59)
  Pallas kernels: 279 us -> 161 us
    pallas_call x1, Pallas kernels: 253 us -> 135 us  [fused(): pl.pallas_call(solve_kernel, out_shape=(jax.ShapeDtypeStruct((COLS - 1, c...]
where the time goes in v2:
time: 170 us
  Pallas kernels  161 us (95%)
  other arithmetic  6 us (4%)
  local copies, waits for them, and re-layouts  2.26 us (1%)
    pallas_call x1, Pallas kernels, fused(): pl.pallas_call(solve_kernel, out_shape=(jax.ShapeDtypeStruct((COLS - 1, c...  135 us
    pallas_call x1, Pallas kernels, fused(): pl.pallas_call(functools.partial(trailing_kernel, heads), grid=(cycles,),...  26.7 us
    convert_element_type x1, other arithmetic, fused(): panel = factor.reshape(cycles, block, width).astype(jnp.bfloat16)  6 us

profile of v2, /device:TPU:0, one launch (start us, length us, event | category | flops | bytes accessed | tf_op | source)
XLA Modules:
  0.0 169.7 jit_solution(13574532093478903320)
XLA Ops:
  0.0 2.3 %slice_bitcast_fusion.grad = bf16[2,256,1024]{2,1,0:T(8,128)(2,1)} fusion(bf16[16,1,256,1024]{3,2,0,1:T(8,128)(2,1)} %bitcast.13), kind=kLoop, calls=%fused_computation.2 | loop fusion | bytes 2097152 | tf_op jit(solution)/shard_map/slice | solution.py:371
  2.3 6.0 %fusion.panel = bf16[16,256,512]{2,1,0:T(8,128)(2,1)} fusion(f32[16,1,256,512]{3,2,1,0:T(8,128)} %param.2), kind=kLoop, calls=%fused_computation.1 | loop fusion | flops 2097152 | bytes 12582912 | tf_op jit(solution)/shard_map/convert_element_type | solution.py:346
  8.3 134.7 %shard_map.28 = (bf16[3,14,256,512]{3,2,1,0:T(8,128)(2,1)}, bf16[4,2048,256]{2,1,0:T(8,128)(2,1)}, f32[2,256,1024]{2,1,0:T(8,128)}) custom-call(bf16[16,256,512]{2,1,0:T(8,128)(2,1)} %fusion.panel, bf16[2,256,1024]{2,1,0:T(8,128)(2,1)} %slice_bitcast_fusion.grad), custom_call_target="tpu_custom_call" | custom-call | tf_op jit(solution)/shard_map/pallas_call | solution.py:351
  143.0 26.7 %shard_map.29 = f32[16,256,1024]{2,1,0:T(8,128)} custom-call(bf16[16,256,512]{2,1,0:T(8,128)(2,1)} %fusion.panel, bf16[3,14,256,512]{3,2,1,0:T(8,128)(2,1)} %get-tuple-element.8.gathered, bf16[4,2048,256]{2,1,0:T(8,128)(2,1)} %get-tuple-element.9.every_solved, f32[2,256,1024]{2,1,0:T(8,128)} %get-tuple-element.10.own_solved, bf16[16,256,1024]{2,1,0:T(8,128)(2,1)} %bitcast.14), custom_call_target="tpu_custom_call" | custom-call | tf_op jit(solution)/shard_map/pallas_call | solution.py:372

commit v3 on v2

--- a/solution.py
+++ b/solution.py
@@ -10,7 +10,7 @@
 STEPS = 8
 ROWS = 4
 COLS = 4
-SPLIT = 4
+SPLIT = 8
 HALF = 128
 GROUP = 2
 MESH = pl.DeviceIdType.MESH
@@ -96,8 +96,8 @@
 
 
 def solve_kernel(
-    panel, grad, gathered, every_solved, own_solved,
-    top, solved, inverse,
+    panel, gradient, gathered, every_solved, own_solved,
+    grad, top, solved, inverse,
     x_send, x_recv, s_send, s_recv, f_send, f_recv,
     up_send, down_send, z_recv, local_sem,
 ):
@@ -170,10 +170,14 @@
     def keep_head(item):
         return pltpu.make_async_copy(panel.at[item], top.at[col, item], local_sem.at[item])
 
+    load_grad = pltpu.make_async_copy(
+        gradient.at[pl.ds(0, heads)], grad, local_sem.at[heads]
+    )
     for item in range(heads):
         to_partner(item).start()
         to_sibling(item).start()
         keep_head(item).start()
+    load_grad.start()
 
     def receive_head(item):
         keep_head(item).wait()
@@ -195,6 +199,7 @@
         to_partner(item).start()
 
     invert(0)
+    load_grad.wait()
     receive_head(1)
 
     @pl.when(row > 0)
@@ -277,14 +282,20 @@
         def _():
             invert(1)
 
-        @pl.when((tick % 3 == 2) & (tick // 3 < groups))
+        @pl.when((tick % 4 == 3) & (tick // 4 < groups))
         def _():
-            pass_on(heads + tick // 3)
-
-    passed = min(groups, ticks // 3)
-
-    write_solved = pltpu.make_async_copy(solved, every_solved, local_sem.at[heads])
-    write_solved.start()
+            pass_on(heads + tick // 4)
+
+    passed = min(groups, ticks // 4)
+
+    def write_solved(part):
+        columns = slice(part * chunk, (part + 1) * chunk)
+        return pltpu.make_async_copy(
+            solved.at[part], every_solved.at[:, columns], local_sem.at[heads + 1 + part]
+        )
+
+    for part in range(SPLIT):
+        write_solved(part).start()
 
     @pl.loop(heads + passed, heads + groups)
     def _(item):
@@ -306,7 +317,8 @@
         def _(part):
             for_sends(position, part, lambda copy: copy.wait_send())
 
-    write_solved.wait()
+    for part in range(SPLIT):
+        write_solved(part).wait()
 
 
 def trailing_kernel(heads, panel, gathered, every_solved, own_solved, grad, out):
@@ -319,19 +331,19 @@
 
     @pl.when(cycle >= heads)
     def _():
-        chunk = every_solved.shape[2]
+        chunk = 2 * HALF
         width = gathered.shape[3]
         sibling = col + 1 - 2 * (col % 2)
         slabs = (col, (col + 2) % COLS, sibling, (sibling + 2) % COLS)
         lefts = (panel[0], gathered[0, 0], gathered[1, 0], gathered[2, 0])
-        for part in range(every_solved.shape[0]):
+        for part in range(every_solved.shape[1] // chunk):
             columns = slice(part * chunk, (part + 1) * chunk)
             total = grad[0, :, columns].astype(jnp.float32)
             product = jnp.zeros(total.shape, jnp.float32)
             for left, slab in zip(lefts, slabs):
                 product = product + jnp.dot(
                     left,
-                    every_solved[part, pl.ds(pl.multiple_of(slab * width, width), width), :],
+                    every_solved[pl.ds(pl.multiple_of(slab * width, width), width), columns],
                     preferred_element_type=jnp.float32,
                 )
             out[0, :, columns] = total - product
@@ -352,23 +364,24 @@
         solve_kernel,
         out_shape=(
             jax.ShapeDtypeStruct((COLS - 1, cycles - heads, block, width), jnp.bfloat16),
-            jax.ShapeDtypeStruct((SPLIT, STEPS * block, chunk), jnp.bfloat16),
+            jax.ShapeDtypeStruct((STEPS * block, columns), jnp.bfloat16),
             jax.ShapeDtypeStruct((heads, block, columns), jnp.float32),
         ),
-        in_specs=[any_spec, vmem_spec],
+        in_specs=[any_spec, any_spec],
         out_specs=(any_spec, any_spec, vmem_spec),
         scratch_shapes=[
+            pltpu.VMEM((heads, block, columns), jnp.bfloat16),
             pltpu.VMEM((COLS, heads, block, width), jnp.bfloat16),
             pltpu.VMEM((SPLIT, STEPS * block, chunk), jnp.bfloat16),
             pltpu.VMEM((heads, 2, HALF, HALF), jnp.float32),
         ]
         + [dma((items,))] * 6
         + [dma((STEPS * SPLIT,))] * 3
-        + [dma((heads + 1,))],
+        + [dma((heads + 1 + SPLIT,))],
         compiler_params=pltpu.CompilerParams(
             collective_id=0, has_side_effects=True, vmem_limit_bytes=56 * 1024 * 1024
         ),
-    )(panel, grad[:heads])
+    )(panel, grad)
     out = pl.pallas_call(
         functools.partial(trailing_kernel, heads),
         grid=(cycles,),
@@ -376,7 +389,7 @@
         in_specs=[
             pl.BlockSpec((1, block, width), lambda i: (jnp.maximum(i, heads), 0, 0)),
             pl.BlockSpec((COLS - 1, 1, block, width), lambda i: (0, jnp.maximum(i - heads, 0), 0, 0)),
-            pl.BlockSpec((SPLIT, STEPS * block, chunk), lambda i: (0, 0, 0)),
+            pl.BlockSpec((STEPS * block, columns), lambda i: (0, 0)),
             pl.BlockSpec((1, block, columns), lambda i: (jnp.minimum(i, heads - 1), 0, 0)),
             pl.BlockSpec((1, block, columns), lambda i: (i, 0, 0)),
         ],

time: 170 us -> 152 us (0.89)
  Pallas kernels: 161 us -> 146 us
  local copies, waits for them, and re-layouts: 2.26 us -> 0 us
    pallas_call x1, Pallas kernels: 135 us -> 119 us  [fused(): pl.pallas_call(solve_kernel, out_shape=(jax.ShapeDtypeStruct((COLS - 1, c...]
    slice x1 -> x0, local copies, waits for them, and re-layouts: 2.26 us -> none  [fused(): grad[:heads]]
where the time goes in v3:
time: 152 us
  Pallas kernels  146 us (96%)
  other arithmetic  6 us (4%)
    pallas_call x1, Pallas kernels, fused(): pl.pallas_call(solve_kernel, out_shape=(jax.ShapeDtypeStruct((COLS - 1, c...  119 us
    pallas_call x1, Pallas kernels, fused(): pl.pallas_call(functools.partial(trailing_kernel, heads), grid=(cycles,),...  26.7 us
    convert_element_type x1, other arithmetic, fused(): panel = factor.reshape(cycles, block, width).astype(jnp.bfloat16)  6 us

profile of v3, /device:TPU:0, one launch (start us, length us, event | category | flops | bytes accessed | tf_op | source)
XLA Modules:
  0.0 151.7 jit_solution(18109103224873907043)
XLA Ops:
  0.0 6.0 %fusion.panel = bf16[16,256,512]{2,1,0:T(8,128)(2,1)} fusion(f32[16,1,256,512]{3,2,1,0:T(8,128)} %param.2), kind=kLoop, calls=%fused_computation.1 | loop fusion | flops 2097152 | bytes 12582912 | tf_op jit(solution)/shard_map/convert_element_type | solution.py:358
  6.0 118.9 %shard_map.28 = (bf16[3,14,256,512]{3,2,1,0:T(8,128)(2,1)}, bf16[2048,1024]{1,0:T(8,128)(2,1)}, f32[2,256,1024]{2,1,0:T(8,128)}) custom-call(bf16[16,256,512]{2,1,0:T(8,128)(2,1)} %fusion.panel, bf16[16,256,1024]{2,1,0:T(8,128)(2,1)} %bitcast.10), custom_call_target="tpu_custom_call" | custom-call | tf_op jit(solution)/shard_map/pallas_call | solution.py:363
  125.0 26.7 %shard_map.29 = f32[16,256,1024]{2,1,0:T(8,128)} custom-call(bf16[16,256,512]{2,1,0:T(8,128)(2,1)} %fusion.panel, bf16[3,14,256,512]{3,2,1,0:T(8,128)(2,1)} %get-tuple-element.8.gathered, bf16[2048,1024]{1,0:T(8,128)(2,1)} %get-tuple-element.9.every_solved, f32[2,256,1024]{2,1,0:T(8,128)} %get-tuple-element.10.own_solved, bf16[16,256,1024]{2,1,0:T(8,128)(2,1)} %bitcast.11), custom_call_target="tpu_custom_call" | custom-call | tf_op jit(solution)/shard_map/pallas_call | solution.py:385

commit v4 on v3

--- a/solution.py
+++ b/solution.py
@@ -323,22 +323,24 @@
 
 def trailing_kernel(heads, panel, gathered, every_solved, own_solved, grad, out):
     col = lax.axis_index("col")
-    cycle = pl.program_id(0)
-
-    @pl.when(cycle < heads)
-    def _():
-        out[0] = own_solved[0]
-
-    @pl.when(cycle >= heads)
+    step = pl.program_id(0)
+
+    @pl.when(step < heads // GROUP)
+    def _():
+        out[...] = own_solved[...]
+
+    @pl.when(step >= heads // GROUP)
     def _():
         chunk = 2 * HALF
         width = gathered.shape[3]
         sibling = col + 1 - 2 * (col % 2)
         slabs = (col, (col + 2) % COLS, sibling, (sibling + 2) % COLS)
-        lefts = (panel[0], gathered[0, 0], gathered[1, 0], gathered[2, 0])
+        height = GROUP * panel.shape[1]
+        lefts = [panel[...].reshape(height, width)]
+        lefts += [gathered[slot].reshape(height, width) for slot in range(COLS - 1)]
         for part in range(every_solved.shape[1] // chunk):
             columns = slice(part * chunk, (part + 1) * chunk)
-            total = grad[0, :, columns].astype(jnp.float32)
+            total = grad[:, :, columns].reshape(height, chunk).astype(jnp.float32)
             product = jnp.zeros(total.shape, jnp.float32)
             for left, slab in zip(lefts, slabs):
                 product = product + jnp.dot(
@@ -346,7 +348,7 @@
                     every_solved[pl.ds(pl.multiple_of(slab * width, width), width), columns],
                     preferred_element_type=jnp.float32,
                 )
-            out[0, :, columns] = total - product
+            out[:, :, columns] = (total - product).reshape(GROUP, height // GROUP, chunk)
 
 
 def fused(factor, gradient):
@@ -384,16 +386,21 @@
     )(panel, grad)
     out = pl.pallas_call(
         functools.partial(trailing_kernel, heads),
-        grid=(cycles,),
+        grid=(cycles // GROUP,),
         out_shape=jax.ShapeDtypeStruct((cycles, block, columns), jnp.float32),
         in_specs=[
-            pl.BlockSpec((1, block, width), lambda i: (jnp.maximum(i, heads), 0, 0)),
-            pl.BlockSpec((COLS - 1, 1, block, width), lambda i: (0, jnp.maximum(i - heads, 0), 0, 0)),
+            pl.BlockSpec((GROUP, block, width), lambda i: (jnp.maximum(i, heads // GROUP), 0, 0)),
+            pl.BlockSpec(
+                (COLS - 1, GROUP, block, width),
+                lambda i: (0, jnp.maximum(i - heads // GROUP, 0), 0, 0),
+            ),
             pl.BlockSpec((STEPS * block, columns), lambda i: (0, 0)),
-            pl.BlockSpec((1, block, columns), lambda i: (jnp.minimum(i, heads - 1), 0, 0)),
-            pl.BlockSpec((1, block, columns), lambda i: (i, 0, 0)),
+            pl.BlockSpec(
+                (GROUP, block, columns), lambda i: (jnp.minimum(i, heads // GROUP - 1), 0, 0)
+            ),
+            pl.BlockSpec((GROUP, block, columns), lambda i: (i, 0, 0)),
         ],
-        out_specs=pl.BlockSpec((1, block, columns), lambda i: (i, 0, 0)),
+        out_specs=pl.BlockSpec((GROUP, block, columns), lambda i: (i, 0, 0)),
         compiler_params=pltpu.CompilerParams(
             dimension_semantics=("arbitrary",), vmem_limit_bytes=56 * 1024 * 1024
         ),
@@ -409,7 +416,8 @@
         and width == 2 * block
         and block == 2 * HALF
         and COLS * width == STEPS * block
-        and (cycles - STEPS // ROWS) % GROUP == 0
+        and cycles % GROUP == 0
+        and STEPS // ROWS % GROUP == 0
     )
     return fused(factor, gradient) if fits else general(factor, gradient)
 

time: 152 us -> 148 us (0.974)
  Pallas kernels: 146 us -> 142 us
    pallas_call x1, Pallas kernels: 26.7 us -> 22.7 us  [fused(): pl.pallas_call(functools.partial(trailing_kernel, heads), grid=(cycles //...]
where the time goes in v4:
time: 148 us
  Pallas kernels  142 us (96%)
  other arithmetic  6 us (4%)
    pallas_call x1, Pallas kernels, fused(): pl.pallas_call(solve_kernel, out_shape=(jax.ShapeDtypeStruct((COLS - 1, c...  119 us
    pallas_call x1, Pallas kernels, fused(): pl.pallas_call(functools.partial(trailing_kernel, heads), grid=(cycles //...  22.7 us
    convert_element_type x1, other arithmetic, fused(): panel = factor.reshape(cycles, block, width).astype(jnp.bfloat16)  6 us

profile of v4, /device:TPU:0, one launch (start us, length us, event | category | flops | bytes accessed | tf_op | source)
XLA Modules:
  0.0 147.7 jit_solution(1778548689197840490)
XLA Ops:
  0.0 6.0 %fusion.panel = bf16[16,256,512]{2,1,0:T(8,128)(2,1)} fusion(f32[16,1,256,512]{3,2,1,0:T(8,128)} %param.2), kind=kLoop, calls=%fused_computation.1 | loop fusion | flops 2097152 | bytes 12582912 | tf_op jit(solution)/shard_map/convert_element_type | solution.py:360
  6.0 118.9 %shard_map.28 = (bf16[3,14,256,512]{3,2,1,0:T(8,128)(2,1)}, bf16[2048,1024]{1,0:T(8,128)(2,1)}, f32[2,256,1024]{2,1,0:T(8,128)}) custom-call(bf16[16,256,512]{2,1,0:T(8,128)(2,1)} %fusion.panel, bf16[16,256,1024]{2,1,0:T(8,128)(2,1)} %bitcast.10), custom_call_target="tpu_custom_call" | custom-call | tf_op jit(solution)/shard_map/pallas_call | solution.py:365
  125.0 22.7 %shard_map.29 = f32[16,256,1024]{2,1,0:T(8,128)} custom-call(bf16[16,256,512]{2,1,0:T(8,128)(2,1)} %fusion.panel, bf16[3,14,256,512]{3,2,1,0:T(8,128)(2,1)} %get-tuple-element.8.gathered, bf16[2048,1024]{1,0:T(8,128)(2,1)} %get-tuple-element.9.every_solved, f32[2,256,1024]{2,1,0:T(8,128)} %get-tuple-element.10.own_solved, bf16[16,256,1024]{2,1,0:T(8,128)(2,1)} %bitcast.11), custom_call_target="tpu_custom_call" | custom-call | tf_op jit(solution)/shard_map/pallas_call | solution.py:387
